TPU v7x, 32 devices: a whole 2x2x4 slice. The times are simulated.
32 devices in a mesh: chain: 8 (over z, core), src: 4 (over y, x).
Axes of the slice: x: 2, y: 2, z: 4, core: 2. Of those that a mesh axis runs over, the one named last changes fastest.
Arguments:
- sources: bfloat16 [256, 4096], P('src', 'chain'), may hold values from -6 to 6
- forward: bfloat16 [256, 4096], P('src', 'chain')
- inv_diag: bfloat16 [8, 512, 512], P('chain'), as said below
- coupling: bfloat16 [8, 2, 512, 512], P('chain'), may hold values from -0.5 to 0.5
- pattern: int32 [8, 2], P('chain'), may hold values 0 or 1
Outputs:
- adjoint: bfloat16 [256, 4096], P('src', 'chain')
- direction: float32 [4096], P('chain')
Inputs may be any that keep to these rules, and one draw needn't show every extreme that they name: inv_diag is the identity plus a dense perturbation of spectral size about one.
All inputs are finite; a program needn't handle non-finite values. No bound on the sum of `pattern` on one device may be relied on, other than what follows from the above.
Results may differ from a plain program's by a relative error of at most 0.02.
Values may be sent and summed in bfloat16 or wider, within the bound.
A program may use at most 64 MiB of HBM per device.

v0:
```python
import jax
import jax.numpy as jnp
from jax import lax
from jax.sharding import PartitionSpec as P


def shifted(x, axis, by):
    devices = lax.axis_size(axis)
    pairs = [(i, i + by) for i in range(devices) if 0 <= i + by < devices]
    return lax.ppermute(x, axis, pairs)


def solve_panel(rows, nearer, farther, inv_block, first_block, second_block, weights):
    first = jnp.dot(nearer, first_block, preferred_element_type=jnp.float32)
    second = jnp.dot(farther, second_block, preferred_element_type=jnp.float32)
    total = rows.astype(jnp.float32) - weights[0] * first - weights[1] * second
    return jnp.dot(
        total.astype(jnp.bfloat16), inv_block, preferred_element_type=jnp.float32
    ).astype(jnp.bfloat16)


def per_device(sources, forward, inv_diag, coupling, pattern):
    chain_size = lax.axis_size("chain")
    inv_block = inv_diag[0]
    first_block = coupling[0, 0]
    second_block = coupling[0, 1]
    weights = pattern[0].astype(jnp.float32)
    src_rows = sources.shape[0]
    width = sources.shape[1]
    zeros_rows = jnp.zeros((src_rows, width), jnp.bfloat16)

    def sweep(step, carry):
        nearer, farther = carry
        solved = solve_panel(
            sources, nearer, farther, inv_block, first_block, second_block, weights
        )
        return shifted((solved, nearer), "chain", -1)

    nearer, farther = lax.fori_loop(0, chain_size - 1, sweep, (zeros_rows, zeros_rows))
    adjoint = solve_panel(sources, nearer, farther, inv_block, first_block, second_block, weights)
    partial_image = jnp.sum(forward.astype(jnp.float32) * adjoint.astype(jnp.float32), axis=0)
    count = float(chain_size * width)
    grad = lax.psum(partial_image, "src")
    squares = lax.psum(jnp.sum(grad * grad), "chain")
    direction = grad / jnp.sqrt(squares / count + 1e-06)
    return (adjoint, direction)


def solution(mesh):
    return jax.shard_map(
        per_device,
        mesh=mesh,
        in_specs=(
            P("src", "chain"),
            P("src", "chain"),
            P("chain", None, None),
            P("chain", None, None, None),
            P("chain", None),
        ),
        out_specs=(P("src", "chain"), P("chain")),
        check_vma=False,
    )
```

profile of v0, /device:TPU:0, one launch (start us, length us, event | category | flops | bytes accessed | tf_op | source)
XLA Modules:
  0.0 103.3 jit_solution(12624970685408298948)
XLA Ops:
  0.6 1.3 %slice_bitcast_fusion = (bf16[512,512]{1,0:T(8,128)(2,1)S(1)}, bf16[512,512]{1,0:T(8,128)(2,1)S(1)}) fusion(bf16[1,2,512,512]{3,2,1,0:T(8,128)(2,1)} %param.10), kind=kLoop, calls=%fused_computation.13 | loop fusion | bytes 2097152 | tf_op jit(solution)/shard_map/squeeze | solution.py:26
  2.0 0.6 copy-done.4
  2.7 0.8 copy-done.2
  3.5 68.3 %while.12 = (s32[]{:T(128)}, bf16[64,512]{1,0:T(8,128)(2,1)S(1)}, bf16[64,512]{1,0:T(8,128)(2,1)S(1)}, bf16[64,512]{1,0:T(8,128)(2,1)S(1)}, f32[2]{0:T(128)S(1)}...) while((s32[]{:T(128)}, bf16[64,512]{1,0:T(8,128)(2,1)S(1)}, ...), condition=%wide.region_1.0_spmd, body=%wide.region_0.0_spmd.sunk | while | flops 100892672 | bytes 2883781 | solution.py:39
  3.5 1.4 %collective-permute-start.1 = (bf16[64,512]{1,0:T(8,128)(2,1)S(1)}, bf16[64,512]{1,0:T(8,128)(2,1)S(1)}, u32[]{:S(2)}, u32[]{:S(2)}) collective-permute-start(bf16[64,512]{1,0:T(8,128)(2,1)S(1)} %copy.11), channel_id=1, source_target_pairs={{4,0},{8,4},{12,8},{16,12},{20,16},{24,20},{28,24},{5,1},{9,5},{13... | collective-permute-start | bytes 196616 | tf_op jit(solution)/shard_map/while/body/eval_jaxpr/ppermute | solution.py:10
  4.9 0.6 fusion.31
  5.5 0.8 fusion.32
  6.3 1.0 convolution_convert_fusion.3
  7.4 1.3 %collective-permute-start = (bf16[64,512]{1,0:T(8,128)(2,1)S(1)}, bf16[64,512]{1,0:T(8,128)(2,1)S(1)}, u32[]{:S(2)}, u32[]{:S(2)}) collective-permute-start(bf16[64,512]{1,0:T(8,128)(2,1)S(1)} %convolution_convert_fusion.3), channel_id=1, source_target_pairs={{4,0},{8,4},{12,8},{16,12},{20,16},{24,20},{28,24},{5,1},{9,5},{13... | collective-permute-start | bytes 196616 | tf_op jit(solution)/shard_map/while/body/eval_jaxpr/ppermute | solution.py:10
  8.7 2.5 %collective-permute-done = bf16[64,512]{1,0:T(8,128)(2,1)S(1)} collective-permute-done((bf16[64,512]{1,0:T(8,128)(2,1)S(1)}, bf16[64,512]{1,0:T(8,128)(2,1)S(1)}, u32[]{:S(2)}, u32[]{:S(2)}) %collective-permute-start) | collective-permute-done | bytes 65568 | tf_op jit(solution)/shard_map/while/body/eval_jaxpr/ppermute | solution.py:10
  11.1 1.3 %collective-permute-start.1 = (bf16[64,512]{1,0:T(8,128)(2,1)S(1)}, bf16[64,512]{1,0:T(8,128)(2,1)S(1)}, u32[]{:S(2)}, u32[]{:S(2)}) collective-permute-start(bf16[64,512]{1,0:T(8,128)(2,1)S(1)} %copy.11), channel_id=1, source_target_pairs={{4,0},{8,4},{12,8},{16,12},{20,16},{24,20},{28,24},{5,1},{9,5},{13... | collective-permute-start | bytes 196616 | tf_op jit(solution)/shard_map/while/body/eval_jaxpr/ppermute | solution.py:10
  13.0 0.8 fusion.32
  13.9 1.0 convolution_convert_fusion.3
  14.9 1.3 %collective-permute-start = (bf16[64,512]{1,0:T(8,128)(2,1)S(1)}, bf16[64,512]{1,0:T(8,128)(2,1)S(1)}, u32[]{:S(2)}, u32[]{:S(2)}) collective-permute-start(bf16[64,512]{1,0:T(8,128)(2,1)S(1)} %convolution_convert_fusion.3), channel_id=1, source_target_pairs={{4,0},{8,4},{12,8},{16,12},{20,16},{24,20},{28,24},{5,1},{9,5},{13... | collective-permute-start | bytes 196616 | tf_op jit(solution)/shard_map/while/body/eval_jaxpr/ppermute | solution.py:10
  16.2 1.4 %collective-permute-done.1 = bf16[64,512]{1,0:T(8,128)(2,1)S(1)} collective-permute-done((bf16[64,512]{1,0:T(8,128)(2,1)S(1)}, bf16[64,512]{1,0:T(8,128)(2,1)S(1)}, u32[]{:S(2)}, u32[]{:S(2)}) %collective-permute-start.1) | collective-permute-done | bytes 65568 | tf_op jit(solution)/shard_map/while/body/eval_jaxpr/ppermute | solution.py:10
  17.6 4.4 %collective-permute-done = bf16[64,512]{1,0:T(8,128)(2,1)S(1)} collective-permute-done((bf16[64,512]{1,0:T(8,128)(2,1)S(1)}, bf16[64,512]{1,0:T(8,128)(2,1)S(1)}, u32[]{:S(2)}, u32[]{:S(2)}) %collective-permute-start) | collective-permute-done | bytes 65568 | tf_op jit(solution)/shard_map/while/body/eval_jaxpr/ppermute | solution.py:10
  22.0 1.3 %collective-permute-start.1 = (bf16[64,512]{1,0:T(8,128)(2,1)S(1)}, bf16[64,512]{1,0:T(8,128)(2,1)S(1)}, u32[]{:S(2)}, u32[]{:S(2)}) collective-permute-start(bf16[64,512]{1,0:T(8,128)(2,1)S(1)} %copy.11), channel_id=1, source_target_pairs={{4,0},{8,4},{12,8},{16,12},{20,16},{24,20},{28,24},{5,1},{9,5},{13... | collective-permute-start | bytes 196616 | tf_op jit(solution)/shard_map/while/body/eval_jaxpr/ppermute | solution.py:10
  23.9 0.8 fusion.32
  24.7 1.0 convolution_convert_fusion.3
  25.8 1.3 %collective-permute-start = (bf16[64,512]{1,0:T(8,128)(2,1)S(1)}, bf16[64,512]{1,0:T(8,128)(2,1)S(1)}, u32[]{:S(2)}, u32[]{:S(2)}) collective-permute-start(bf16[64,512]{1,0:T(8,128)(2,1)S(1)} %convolution_convert_fusion.3), channel_id=1, source_target_pairs={{4,0},{8,4},{12,8},{16,12},{20,16},{24,20},{28,24},{5,1},{9,5},{13... | collective-permute-start | bytes 196616 | tf_op jit(solution)/shard_map/while/body/eval_jaxpr/ppermute | solution.py:10
  27.6 4.4 %collective-permute-done = bf16[64,512]{1,0:T(8,128)(2,1)S(1)} collective-permute-done((bf16[64,512]{1,0:T(8,128)(2,1)S(1)}, bf16[64,512]{1,0:T(8,128)(2,1)S(1)}, u32[]{:S(2)}, u32[]{:S(2)}) %collective-permute-start) | collective-permute-done | bytes 65568 | tf_op jit(solution)/shard_map/while/body/eval_jaxpr/ppermute | solution.py:10
  32.0 1.3 %collective-permute-start.1 = (bf16[64,512]{1,0:T(8,128)(2,1)S(1)}, bf16[64,512]{1,0:T(8,128)(2,1)S(1)}, u32[]{:S(2)}, u32[]{:S(2)}) collective-permute-start(bf16[64,512]{1,0:T(8,128)(2,1)S(1)} %copy.11), channel_id=1, source_target_pairs={{4,0},{8,4},{12,8},{16,12},{20,16},{24,20},{28,24},{5,1},{9,5},{13... | collective-permute-start | bytes 196616 | tf_op jit(solution)/shard_map/while/body/eval_jaxpr/ppermute | solution.py:10
  33.3 0.6 fusion.31
  33.8 0.8 fusion.32
  34.7 1.0 convolution_convert_fusion.3
  35.7 1.3 %collective-permute-start = (bf16[64,512]{1,0:T(8,128)(2,1)S(1)}, bf16[64,512]{1,0:T(8,128)(2,1)S(1)}, u32[]{:S(2)}, u32[]{:S(2)}) collective-permute-start(bf16[64,512]{1,0:T(8,128)(2,1)S(1)} %convolution_convert_fusion.3), channel_id=1, source_target_pairs={{4,0},{8,4},{12,8},{16,12},{20,16},{24,20},{28,24},{5,1},{9,5},{13... | collective-permute-start | bytes 196616 | tf_op jit(solution)/shard_map/while/body/eval_jaxpr/ppermute | solution.py:10
  37.6 4.4 %collective-permute-done = bf16[64,512]{1,0:T(8,128)(2,1)S(1)} collective-permute-done((bf16[64,512]{1,0:T(8,128)(2,1)S(1)}, bf16[64,512]{1,0:T(8,128)(2,1)S(1)}, u32[]{:S(2)}, u32[]{:S(2)}) %collective-permute-start) | collective-permute-done | bytes 65568 | tf_op jit(solution)/shard_map/while/body/eval_jaxpr/ppermute | solution.py:10
  41.9 1.3 %collective-permute-start.1 = (bf16[64,512]{1,0:T(8,128)(2,1)S(1)}, bf16[64,512]{1,0:T(8,128)(2,1)S(1)}, u32[]{:S(2)}, u32[]{:S(2)}) collective-permute-start(bf16[64,512]{1,0:T(8,128)(2,1)S(1)} %copy.11), channel_id=1, source_target_pairs={{4,0},{8,4},{12,8},{16,12},{20,16},{24,20},{28,24},{5,1},{9,5},{13... | collective-permute-start | bytes 196616 | tf_op jit(solution)/shard_map/while/body/eval_jaxpr/ppermute | solution.py:10
  43.8 0.8 fusion.32
  44.7 1.0 convolution_convert_fusion.3
  45.7 1.3 %collective-permute-start = (bf16[64,512]{1,0:T(8,128)(2,1)S(1)}, bf16[64,512]{1,0:T(8,128)(2,1)S(1)}, u32[]{:S(2)}, u32[]{:S(2)}) collective-permute-start(bf16[64,512]{1,0:T(8,128)(2,1)S(1)} %convolution_convert_fusion.3), channel_id=1, source_target_pairs={{4,0},{8,4},{12,8},{16,12},{20,16},{24,20},{28,24},{5,1},{9,5},{13... | collective-permute-start | bytes 196616 | tf_op jit(solution)/shard_map/while/body/eval_jaxpr/ppermute | solution.py:10
  47.5 4.4 %collective-permute-done = bf16[64,512]{1,0:T(8,128)(2,1)S(1)} collective-permute-done((bf16[64,512]{1,0:T(8,128)(2,1)S(1)}, bf16[64,512]{1,0:T(8,128)(2,1)S(1)}, u32[]{:S(2)}, u32[]{:S(2)}) %collective-permute-start) | collective-permute-done | bytes 65568 | tf_op jit(solution)/shard_map/while/body/eval_jaxpr/ppermute | solution.py:10
  51.9 1.3 %collective-permute-start.1 = (bf16[64,512]{1,0:T(8,128)(2,1)S(1)}, bf16[64,512]{1,0:T(8,128)(2,1)S(1)}, u32[]{:S(2)}, u32[]{:S(2)}) collective-permute-start(bf16[64,512]{1,0:T(8,128)(2,1)S(1)} %copy.11), channel_id=1, source_target_pairs={{4,0},{8,4},{12,8},{16,12},{20,16},{24,20},{28,24},{5,1},{9,5},{13... | collective-permute-start | bytes 196616 | tf_op jit(solution)/shard_map/while/body/eval_jaxpr/ppermute | solution.py:10
  53.8 0.8 fusion.32
  54.6 1.0 convolution_convert_fusion.3
  55.6 1.3 %collective-permute-start = (bf16[64,512]{1,0:T(8,128)(2,1)S(1)}, bf16[64,512]{1,0:T(8,128)(2,1)S(1)}, u32[]{:S(2)}, u32[]{:S(2)}) collective-permute-start(bf16[64,512]{1,0:T(8,128)(2,1)S(1)} %convolution_convert_fusion.3), channel_id=1, source_target_pairs={{4,0},{8,4},{12,8},{16,12},{20,16},{24,20},{28,24},{5,1},{9,5},{13... | collective-permute-start | bytes 196616 | tf_op jit(solution)/shard_map/while/body/eval_jaxpr/ppermute | solution.py:10
  57.5 4.4 %collective-permute-done = bf16[64,512]{1,0:T(8,128)(2,1)S(1)} collective-permute-done((bf16[64,512]{1,0:T(8,128)(2,1)S(1)}, bf16[64,512]{1,0:T(8,128)(2,1)S(1)}, u32[]{:S(2)}, u32[]{:S(2)}) %collective-permute-start) | collective-permute-done | bytes 65568 | tf_op jit(solution)/shard_map/while/body/eval_jaxpr/ppermute | solution.py:10
  61.9 1.3 %collective-permute-start.1 = (bf16[64,512]{1,0:T(8,128)(2,1)S(1)}, bf16[64,512]{1,0:T(8,128)(2,1)S(1)}, u32[]{:S(2)}, u32[]{:S(2)}) collective-permute-start(bf16[64,512]{1,0:T(8,128)(2,1)S(1)} %copy.11), channel_id=1, source_target_pairs={{4,0},{8,4},{12,8},{16,12},{20,16},{24,20},{28,24},{5,1},{9,5},{13... | collective-permute-start | bytes 196616 | tf_op jit(solution)/shard_map/while/body/eval_jaxpr/ppermute | solution.py:10
  63.7 0.8 fusion.32
  64.6 1.0 convolution_convert_fusion.3
  65.6 1.3 %collective-permute-start = (bf16[64,512]{1,0:T(8,128)(2,1)S(1)}, bf16[64,512]{1,0:T(8,128)(2,1)S(1)}, u32[]{:S(2)}, u32[]{:S(2)}) collective-permute-start(bf16[64,512]{1,0:T(8,128)(2,1)S(1)} %convolution_convert_fusion.3), channel_id=1, source_target_pairs={{4,0},{8,4},{12,8},{16,12},{20,16},{24,20},{28,24},{5,1},{9,5},{13... | collective-permute-start | bytes 196616 | tf_op jit(solution)/shard_map/while/body/eval_jaxpr/ppermute | solution.py:10
  67.4 4.4 %collective-permute-done = bf16[64,512]{1,0:T(8,128)(2,1)S(1)} collective-permute-done((bf16[64,512]{1,0:T(8,128)(2,1)S(1)}, bf16[64,512]{1,0:T(8,128)(2,1)S(1)}, u32[]{:S(2)}, u32[]{:S(2)}) %collective-permute-start) | collective-permute-done | bytes 65568 | tf_op jit(solution)/shard_map/while/body/eval_jaxpr/ppermute | solution.py:10
  72.4 0.9 fusion.5
  73.3 1.7 %multiply_reduce_fusion = (f32[512]{0:T(512)S(1)}, bf16[64,512]{1,0:T(8,128)(2,1)}) fusion(bf16[64,512]{1,0:T(8,128)(2,1)S(1)} %copy-done.3, bf16[1,512,512]{2,1,0:T(8,128)(2,1)S(1)} %bitcast.42, f32[64,512]{1,0:T(8,128)S(1)} %fusion.5, bf16[64,512]{1,0:T(8,128)(2,1)S(1)} %get-tuple-element.46, f32[]{:T(128)} %bitcast.7, ...), kind=kOutput, calls=%fused_computation.15 | convolution fusion | flops 67370496 | bytes 1378308 | tf_op jit(solution)/shard_map/dot_general | solution.py:17
  74.9 10.4 %psum.14 = f32[512]{0:T(512)S(1)} all-reduce(f32[512]{0:T(512)S(1)} %get-tuple-element.71), channel_id=1, replica_groups=mesh['chain'=8,'src'=4] {'src'}, use_global_device_ids=true, to_apply=%region_3.0 | all-reduce | flops 512 | bytes 4096 | tf_op jit(solution)/shard_map/psum | solution.py:43
  85.4 0.6 multiply_reduce_fusion.1
  86.0 16.1 %psum.15 = f32[]{:T(128)} all-reduce(f32[]{:T(128)} %multiply_reduce_fusion.1), channel_id=1, replica_groups=mesh['chain'=8,'src'=4] {'chain'}, use_global_device_ids=true, to_apply=%region_5.0 | all-reduce | flops 1 | bytes 8 | tf_op jit(solution)/shard_map/psum | solution.py:44
  102.7 0.6 broadcast_divide_fusion
  (37 shorter events, 6.3 us)
Async XLA Ops:
  0.6 2.0 %copy-start = (bf16[1,512,512]{2,1,0:T(8,128)(2,1)S(1)}, bf16[1,512,512]{2,1,0:T(8,128)(2,1)}, u32[]{:S(2)}) copy-start(bf16[1,512,512]{2,1,0:T(8,128)(2,1)} %param.9) | copy-start | bytes 1572868
  2.0 0.7 copy-start.4
  2.6 0.8 copy-start.2
  3.5 68.9 %copy-start.1 = (bf16[1,2,512,512]{3,2,1,0:T(8,128)(2,1)S(1)}, bf16[1,2,512,512]{3,2,1,0:T(8,128)(2,1)}, u32[]{:S(2)}) copy-start(bf16[1,2,512,512]{3,2,1,0:T(8,128)(2,1)} %param.10) | copy-start | bytes 3145732
  3.5 5.2 %collective-permute-start.1 = (bf16[64,512]{1,0:T(8,128)(2,1)S(1)}, bf16[64,512]{1,0:T(8,128)(2,1)S(1)}, u32[]{:S(2)}, u32[]{:S(2)}) collective-permute-start(bf16[64,512]{1,0:T(8,128)(2,1)S(1)} %copy.11), channel_id=1, source_target_pairs={{4,0},{8,4},{12,8},{16,12},{20,16},{24,20},{28,24},{5,1},{9,5},{13... | collective-permute-start | bytes 196616 | tf_op jit(solution)/shard_map/while/body/eval_jaxpr/ppermute | solution.py:10
  7.4 3.8 %collective-permute-start = (bf16[64,512]{1,0:T(8,128)(2,1)S(1)}, bf16[64,512]{1,0:T(8,128)(2,1)S(1)}, u32[]{:S(2)}, u32[]{:S(2)}) collective-permute-start(bf16[64,512]{1,0:T(8,128)(2,1)S(1)} %convolution_convert_fusion.3), channel_id=1, source_target_pairs={{4,0},{8,4},{12,8},{16,12},{20,16},{24,20},{28,24},{5,1},{9,5},{13... | collective-permute-start | bytes 196616 | tf_op jit(solution)/shard_map/while/body/eval_jaxpr/ppermute | solution.py:10
  11.1 6.5 %collective-permute-start.1 = (bf16[64,512]{1,0:T(8,128)(2,1)S(1)}, bf16[64,512]{1,0:T(8,128)(2,1)S(1)}, u32[]{:S(2)}, u32[]{:S(2)}) collective-permute-start(bf16[64,512]{1,0:T(8,128)(2,1)S(1)} %copy.11), channel_id=1, source_target_pairs={{4,0},{8,4},{12,8},{16,12},{20,16},{24,20},{28,24},{5,1},{9,5},{13... | collective-permute-start | bytes 196616 | tf_op jit(solution)/shard_map/while/body/eval_jaxpr/ppermute | solution.py:10
  14.9 7.1 %collective-permute-start = (bf16[64,512]{1,0:T(8,128)(2,1)S(1)}, bf16[64,512]{1,0:T(8,128)(2,1)S(1)}, u32[]{:S(2)}, u32[]{:S(2)}) collective-permute-start(bf16[64,512]{1,0:T(8,128)(2,1)S(1)} %convolution_convert_fusion.3), channel_id=1, source_target_pairs={{4,0},{8,4},{12,8},{16,12},{20,16},{24,20},{28,24},{5,1},{9,5},{13... | collective-permute-start | bytes 196616 | tf_op jit(solution)/shard_map/while/body/eval_jaxpr/ppermute | solution.py:10
  22.0 5.6 %collective-permute-start.1 = (bf16[64,512]{1,0:T(8,128)(2,1)S(1)}, bf16[64,512]{1,0:T(8,128)(2,1)S(1)}, u32[]{:S(2)}, u32[]{:S(2)}) collective-permute-start(bf16[64,512]{1,0:T(8,128)(2,1)S(1)} %copy.11), channel_id=1, source_target_pairs={{4,0},{8,4},{12,8},{16,12},{20,16},{24,20},{28,24},{5,1},{9,5},{13... | collective-permute-start | bytes 196616 | tf_op jit(solution)/shard_map/while/body/eval_jaxpr/ppermute | solution.py:10
  25.8 6.2 %collective-permute-start = (bf16[64,512]{1,0:T(8,128)(2,1)S(1)}, bf16[64,512]{1,0:T(8,128)(2,1)S(1)}, u32[]{:S(2)}, u32[]{:S(2)}) collective-permute-start(bf16[64,512]{1,0:T(8,128)(2,1)S(1)} %convolution_convert_fusion.3), channel_id=1, source_target_pairs={{4,0},{8,4},{12,8},{16,12},{20,16},{24,20},{28,24},{5,1},{9,5},{13... | collective-permute-start | bytes 196616 | tf_op jit(solution)/shard_map/while/body/eval_jaxpr/ppermute | solution.py:10
  32.0 5.6 %collective-permute-start.1 = (bf16[64,512]{1,0:T(8,128)(2,1)S(1)}, bf16[64,512]{1,0:T(8,128)(2,1)S(1)}, u32[]{:S(2)}, u32[]{:S(2)}) collective-permute-start(bf16[64,512]{1,0:T(8,128)(2,1)S(1)} %copy.11), channel_id=1, source_target_pairs={{4,0},{8,4},{12,8},{16,12},{20,16},{24,20},{28,24},{5,1},{9,5},{13... | collective-permute-start | bytes 196616 | tf_op jit(solution)/shard_map/while/body/eval_jaxpr/ppermute | solution.py:10
  35.7 6.2 %collective-permute-start = (bf16[64,512]{1,0:T(8,128)(2,1)S(1)}, bf16[64,512]{1,0:T(8,128)(2,1)S(1)}, u32[]{:S(2)}, u32[]{:S(2)}) collective-permute-start(bf16[64,512]{1,0:T(8,128)(2,1)S(1)} %convolution_convert_fusion.3), channel_id=1, source_target_pairs={{4,0},{8,4},{12,8},{16,12},{20,16},{24,20},{28,24},{5,1},{9,5},{13... | collective-permute-start | bytes 196616 | tf_op jit(solution)/shard_map/while/body/eval_jaxpr/ppermute | solution.py:10
  41.9 5.6 %collective-permute-start.1 = (bf16[64,512]{1,0:T(8,128)(2,1)S(1)}, bf16[64,512]{1,0:T(8,128)(2,1)S(1)}, u32[]{:S(2)}, u32[]{:S(2)}) collective-permute-start(bf16[64,512]{1,0:T(8,128)(2,1)S(1)} %copy.11), channel_id=1, source_target_pairs={{4,0},{8,4},{12,8},{16,12},{20,16},{24,20},{28,24},{5,1},{9,5},{13... | collective-permute-start | bytes 196616 | tf_op jit(solution)/shard_map/while/body/eval_jaxpr/ppermute | solution.py:10
  45.7 6.2 %collective-permute-start = (bf16[64,512]{1,0:T(8,128)(2,1)S(1)}, bf16[64,512]{1,0:T(8,128)(2,1)S(1)}, u32[]{:S(2)}, u32[]{:S(2)}) collective-permute-start(bf16[64,512]{1,0:T(8,128)(2,1)S(1)} %convolution_convert_fusion.3), channel_id=1, source_target_pairs={{4,0},{8,4},{12,8},{16,12},{20,16},{24,20},{28,24},{5,1},{9,5},{13... | collective-permute-start | bytes 196616 | tf_op jit(solution)/shard_map/while/body/eval_jaxpr/ppermute | solution.py:10
  51.9 5.6 %collective-permute-start.1 = (bf16[64,512]{1,0:T(8,128)(2,1)S(1)}, bf16[64,512]{1,0:T(8,128)(2,1)S(1)}, u32[]{:S(2)}, u32[]{:S(2)}) collective-permute-start(bf16[64,512]{1,0:T(8,128)(2,1)S(1)} %copy.11), channel_id=1, source_target_pairs={{4,0},{8,4},{12,8},{16,12},{20,16},{24,20},{28,24},{5,1},{9,5},{13... | collective-permute-start | bytes 196616 | tf_op jit(solution)/shard_map/while/body/eval_jaxpr/ppermute | solution.py:10
  55.6 6.2 %collective-permute-start = (bf16[64,512]{1,0:T(8,128)(2,1)S(1)}, bf16[64,512]{1,0:T(8,128)(2,1)S(1)}, u32[]{:S(2)}, u32[]{:S(2)}) collective-permute-start(bf16[64,512]{1,0:T(8,128)(2,1)S(1)} %convolution_convert_fusion.3), channel_id=1, source_target_pairs={{4,0},{8,4},{12,8},{16,12},{20,16},{24,20},{28,24},{5,1},{9,5},{13... | collective-permute-start | bytes 196616 | tf_op jit(solution)/shard_map/while/body/eval_jaxpr/ppermute | solution.py:10
  61.9 5.6 %collective-permute-start.1 = (bf16[64,512]{1,0:T(8,128)(2,1)S(1)}, bf16[64,512]{1,0:T(8,128)(2,1)S(1)}, u32[]{:S(2)}, u32[]{:S(2)}) collective-permute-start(bf16[64,512]{1,0:T(8,128)(2,1)S(1)} %copy.11), channel_id=1, source_target_pairs={{4,0},{8,4},{12,8},{16,12},{20,16},{24,20},{28,24},{5,1},{9,5},{13... | collective-permute-start | bytes 196616 | tf_op jit(solution)/shard_map/while/body/eval_jaxpr/ppermute | solution.py:10
  65.6 6.2 %collective-permute-start = (bf16[64,512]{1,0:T(8,128)(2,1)S(1)}, bf16[64,512]{1,0:T(8,128)(2,1)S(1)}, u32[]{:S(2)}, u32[]{:S(2)}) collective-permute-start(bf16[64,512]{1,0:T(8,128)(2,1)S(1)} %convolution_convert_fusion.3), channel_id=1, source_target_pairs={{4,0},{8,4},{12,8},{16,12},{20,16},{24,20},{28,24},{5,1},{9,5},{13... | collective-permute-start | bytes 196616 | tf_op jit(solution)/shard_map/while/body/eval_jaxpr/ppermute | solution.py:10
  72.4 0.9 copy-start.3
where the time goes:
time: 104 us; the launch traced here: 103 us
  waiting for transfers between devices  32.8 us (32%)
  blocking collectives  26.5 us (25%)
  starting transfers between devices  18.2 us (18%)
  matrix products  15.5 us (15%)
  local copies, waits for them, and re-layouts  7.55 us (7%)
  between operations  1.38 us (1%)
  other arithmetic  1.19 us (1%)
    ppermute x14, waiting for transfers between devices, shifted(): return lax.ppermute(x, axis, pairs)  32.8 us
    ppermute x14, starting transfers between devices, shifted(): return lax.ppermute(x, axis, pairs)  18.2 us
    psum x1, blocking collectives, per_device(): squares = lax.psum(jnp.sum(grad * grad), 'chain')  16.1 us
    psum x1, blocking collectives, per_device(): grad = lax.psum(partial_image, 'src')  10.4 us
    dot_general x8, matrix products, solve_panel(): jnp.dot(total.astype(jnp.bfloat16), inv_block, preferred_element_type=jnp...  8.74 us
    dot_general x8, matrix products, solve_panel(): first = jnp.dot(nearer, first_block, preferred_element_type=jnp.float32)  6.75 us
    slice x8, local copies, waits for them, and re-layouts, solve_panel(): total = rows.astype(jnp.float32) - weights[0] * first - weights[1] * second  4.67 us
  transfers between devices with their start and end apart: 14, of which 13 were waited for; matrix products, arithmetic and copies ran while one was open for 17% of the time, Pallas kernels for 0%

commit v1 on v0

v1 whole, which is shorter than its diff:
```python
import functools

import jax
import jax.numpy as jnp
from jax import lax
from jax.experimental import pallas as pl
from jax.experimental.pallas import tpu as pltpu
from jax.sharding import PartitionSpec as P

F32 = jnp.float32
BF16 = jnp.bfloat16
MESH = pl.DeviceIdType.MESH


def matmul(a, b):
    return jnp.dot(a, b, preferred_element_type=F32)


def kernel(n, groups, pattern, sources, forward, inv_diag, coupling, adjoint, direction,
           rows, waves, inv, blocks, base, near_mat, far_mat, near, far, solved, parts, squares,
           load_sem, store_sem, send_sem, near_sem, far_sem, part_send, part_recv, sq_send, sq_recv):
    k = lax.axis_index("chain")
    g = lax.axis_index("src")
    odd = lax.rem(k, 2) == 1

    loads = [
        pltpu.make_async_copy(inv_diag.at[0], inv, load_sem.at[0]),
        pltpu.make_async_copy(sources, rows, load_sem.at[1]),
        pltpu.make_async_copy(coupling.at[0, 0], blocks.at[0], load_sem.at[2]),
        pltpu.make_async_copy(coupling.at[0, 1], blocks.at[1], load_sem.at[3]),
        pltpu.make_async_copy(forward, waves, load_sem.at[4]),
    ]
    for load in loads:
        load.start()

    barrier = pltpu.get_barrier_semaphore()
    for step in range(1, n):
        pl.semaphore_signal(barrier, inc=1, device_id=(lax.rem(k + step, n), g), device_id_type=MESH)
    for step in range(1, groups):
        pl.semaphore_signal(barrier, inc=1, device_id=(k, lax.rem(g + step, groups)), device_id_type=MESH)

    def remote(src, dst, send, recv, chain_to, src_to):
        return pltpu.make_async_remote_copy(
            src_ref=src, dst_ref=dst, send_sem=send, recv_sem=recv,
            device_id=(chain_to, src_to), device_id_type=MESH,
        )

    one_down = lax.max(k - 1, 0)
    two_down = lax.max(k - 2, 0)
    to_near = remote(solved, near, send_sem.at[0], near_sem, one_down, g)
    to_far = remote(solved, far, send_sem.at[1], far_sem, two_down, g)
    onward = remote(near, far, send_sem.at[2], far_sem, one_down, g)

    loads[0].wait()
    loads[1].wait()
    base[...] = matmul(rows[...], inv[...])
    pl.semaphore_wait(barrier, n - 1 + groups - 1)

    loads[2].wait()
    loads[3].wait()

    @pl.when(k < n - 1)
    def _():
        near_mat[...] = (matmul(blocks[0], inv[...]) * -pattern[0, 0].astype(F32)).astype(BF16)

    @pl.when(k < n - 2)
    def _():
        far_mat[...] = (matmul(blocks[1], inv[...]) * -pattern[0, 1].astype(F32)).astype(BF16)
        to_far.wait_recv()
        base[...] += matmul(far[...], far_mat[...])

    @pl.when(k < n - 1)
    def _():
        to_near.wait_recv()

        @pl.when(odd)
        def _():
            onward.start()

        solved[...] = (base[...] + matmul(near[...], near_mat[...])).astype(BF16)

    @pl.when(k == n - 1)
    def _():
        solved[...] = base[...].astype(BF16)

    @pl.when(k > 0)
    def _():
        to_near.start()

    @pl.when(odd & (k > 1))
    def _():
        to_far.start()

    store = pltpu.make_async_copy(solved, adjoint, store_sem)
    store.start()

    loads[4].wait()
    parts[g] = jnp.sum(waves[...].astype(F32) * solved[...].astype(F32), axis=0, keepdims=True)

    def part_copy(step, owner):
        return remote(parts.at[owner], parts.at[owner], part_send.at[step], part_recv.at[owner],
                      k, lax.rem(g + step, groups))

    for step in range(1, groups):
        part_copy(step, g).start()
    for step in range(1, groups):
        part_copy(step, lax.rem(g + groups - step, groups)).wait_recv()
    grad = parts[0]
    for group in range(1, groups):
        grad = grad + parts[group]
    squares[k] = jnp.broadcast_to(jnp.sum(grad * grad, axis=1, keepdims=True), (1, 128))

    def square_copy(step, owner):
        return remote(squares.at[owner], squares.at[owner], sq_send.at[step], sq_recv.at[owner],
                      lax.rem(k + step, n), g)

    for step in range(1, n):
        square_copy(step, k).start()
    for step in range(1, n):
        square_copy(step, lax.rem(k + n - step, n)).wait_recv()
    total = squares[0]
    for panel in range(1, n):
        total = total + squares[panel]
    count = float(n * grad.shape[1])
    scale = jnp.sqrt(total / count + 1e-06)
    direction[...] = grad / jnp.broadcast_to(scale[:, :1], grad.shape)

    for step in range(1, groups):
        part_copy(step, g).wait_send()
    for step in range(1, n):
        square_copy(step, k).wait_send()

    @pl.when(k > 0)
    def _():
        to_near.wait_send()

    @pl.when(odd & (k > 1))
    def _():
        to_far.wait_send()

    @pl.when(odd & (k < n - 1))
    def _():
        onward.wait_send()

    store.wait()


def solution(mesh):
    n = mesh.shape["chain"]
    groups = mesh.shape["src"]

    def per_device(sources, forward, inv_diag, coupling, pattern):
        count, width = sources.shape
        anywhere = pl.BlockSpec(memory_space=pl.ANY)
        adjoint, direction = pl.pallas_call(
            functools.partial(kernel, n, groups),
            out_shape=(
                jax.ShapeDtypeStruct((count, width), BF16),
                jax.ShapeDtypeStruct((1, width), F32),
            ),
            in_specs=[pl.BlockSpec(memory_space=pltpu.SMEM)] + [anywhere] * 4,
            out_specs=(anywhere, pl.BlockSpec(memory_space=pltpu.VMEM)),
            scratch_shapes=[
                pltpu.VMEM((count, width), BF16),
                pltpu.VMEM((count, width), BF16),
                pltpu.VMEM((width, width), BF16),
                pltpu.VMEM((2, width, width), BF16),
                pltpu.VMEM((count, width), F32),
                pltpu.VMEM((width, width), BF16),
                pltpu.VMEM((width, width), BF16),
                pltpu.VMEM((count, width), BF16),
                pltpu.VMEM((count, width), BF16),
                pltpu.VMEM((count, width), BF16),
                pltpu.VMEM((groups, 1, width), F32),
                pltpu.VMEM((n, 1, 128), F32),
                pltpu.SemaphoreType.DMA((5,)),
                pltpu.SemaphoreType.DMA,
                pltpu.SemaphoreType.DMA((3,)),
                pltpu.SemaphoreType.DMA,
                pltpu.SemaphoreType.DMA,
                pltpu.SemaphoreType.DMA((groups,)),
                pltpu.SemaphoreType.DMA((groups,)),
                pltpu.SemaphoreType.DMA((n,)),
                pltpu.SemaphoreType.DMA((n,)),
            ],
            compiler_params=pltpu.CompilerParams(
                collective_id=0, has_side_effects=True, vmem_limit_bytes=60 * 1024 * 1024
            ),
            cost_estimate=pl.CostEstimate(
                flops=2 * width * width * (2 * width + 3 * count),
                bytes_accessed=6 * width * width + 6 * count * width,
                transcendentals=0,
            ),
        )(pattern, sources, forward, inv_diag, coupling)
        return adjoint, direction.reshape(width)

    return jax.shard_map(
        per_device,
        mesh=mesh,
        in_specs=(
            P("src", "chain"),
            P("src", "chain"),
            P("chain", None, None),
            P("chain", None, None, None),
            P("chain", None),
        ),
        out_specs=(P("src", "chain"), P("chain")),
        check_vma=False,
    )
```

time: 104 us -> 28.2 us (0.27)
  waiting for transfers between devices: 32.8 us -> 0 us
  blocking collectives: 26.5 us -> 0 us
  Pallas kernels: 0 us -> 25.3 us
  starting transfers between devices: 18.2 us -> 0 us
  matrix products: 15.5 us -> 0 us
  local copies, waits for them, and re-layouts: 7.55 us -> 2.06 us
  other arithmetic: 1.19 us -> 0 us
    ppermute x14 -> x0, waiting for transfers between devices: 32.8 us -> none  [shifted(): return lax.ppermute(x, axis, pairs)]
    psum x2 -> x0, blocking collectives: 26.5 us -> none  [the longest x1 16.1 us: per_device(): squares = lax.psum(jnp.sum(grad * grad), 'chain')]
    pallas_call x0 -> x1, Pallas kernels: none -> 25.3 us  [per_device(): pl.pallas_call(functools.partial(kernel, n, groups), out_shape=(jax.Shape...]
    ppermute x14 -> x0, starting transfers between devices: 18.2 us -> none  [shifted(): return lax.ppermute(x, axis, pairs)]
    dot_general x16 -> x0, matrix products: 15.5 us -> none  [the longest x8 8.74 us: solve_panel(): jnp.dot(total.astype(jnp.bfloat16), inv_block, preferred_element_type=jnp...]
    slice x8 -> x0, local copies, waits for them, and re-layouts: 4.67 us -> none  [solve_panel(): total = rows.astype(jnp.float32) - weights[0] * first - weights[1] * second]
    squeeze x1 -> x0, local copies, waits for them, and re-layouts: 1.33 us -> none  [per_device(): second_block = coupling[0, 1]]
  transfers between devices with their start and end apart: 14 -> 0, of which waited for: 13 -> 0; matrix products, arithmetic and copies ran while one was open for 17% -> 0% of each run, Pallas kernels for 0% -> 0%
where the time goes in v1:
time: 28.2 us; the launch traced here: 28 us
  Pallas kernels  25.3 us (90%)
  local copies, waits for them, and re-layouts  2.06 us (7%)
  between operations  0.65 us (2%)
    pallas_call x1, Pallas kernels, per_device(): pl.pallas_call(functools.partial(kernel, n, groups), out_shape=(jax.Shape...  25.3 us
    unnamed x4, local copies, waits for them, and re-layouts  2.06 us

profile of v1, /device:TPU:0, one launch (start us, length us, event | category | flops | bytes accessed | tf_op | source)
XLA Modules:
  0.0 28.0 jit_solution(9459711566670941901)
XLA Ops:
  0.6 25.3 %shard_map.68 = (bf16[64,512]{1,0:T(8,128)(2,1)}, f32[1,512]{1,0:T(1,128)}) custom-call(s32[1,2]{1,0:T(1,128)} %pattern.1, bf16[64,512]{1,0:T(8,128)(2,1)} %sources.1, bf16[64,512]{1,0:T(8,128)(2,1)} %forward.1, bf16[1,512,512]{2,1,0:T(8,128)(2,1)} %inv_diag.1, bf16[1,2,512,512]{3,2,1,0:T(8,128)(2,1)} %coupling.1), custom_call_target="tpu_custom_call" | custom-call | flops 637534208 | bytes 1769472 | tf_op jit(solution)/shard_map/pallas_call | solution.py:155
  25.9 0.0 copy-start
  25.9 1.5 %copy.9 = bf16[64,512]{1,0:T(8,128)(2,1)} copy(bf16[64,512]{1,0:T(8,128)(2,1)} %get-tuple-element.8) | data formatting | bytes 131072
  27.4 0.0 copy-done
  27.4 0.6 %copy.10 = f32[512]{0:T(512)} copy(f32[512]{0:T(512)S(1)} %bitcast.1) | data formatting | bytes 4096
Async XLA Ops:
  25.9 1.5 %copy-start = (f32[1,512]{1,0:T(1,128)S(1)}, f32[1,512]{1,0:T(1,128)}, u32[]{:S(2)}) copy-start(f32[1,512]{1,0:T(1,128)} %get-tuple-element.5) | copy-start | bytes 6148

commit v2 on v1

v2 whole, which is shorter than its diff:
```python
import functools

import jax
import jax.numpy as jnp
from jax import lax
from jax.experimental import pallas as pl
from jax.experimental.pallas import tpu as pltpu
from jax.sharding import PartitionSpec as P

F32 = jnp.float32
BF16 = jnp.bfloat16
MESH = pl.DeviceIdType.MESH


def matmul(a, b):
    return jnp.dot(a, b, preferred_element_type=F32)


def kernel(n, groups, pattern, sources, forward, inv_diag, coupling, adjoint, direction,
           rows, waves, inv, blocks, base, mats, above, solved, mine_part, parts, squares,
           load_sem, store_sem, pair_send, pair_recv, down_send, down_recv, back_send, back_recv,
           part_send, part_recv, sq_send, sq_recv):
    k = lax.axis_index("chain")
    g = lax.axis_index("src")
    c = lax.rem(k, 2)
    first = k - c
    peer = first + 1 - c
    top = k >= n - 2
    bottom = k < 2
    half = rows.shape[0] // 2
    mine = pl.ds(pl.multiple_of(c * half, half), half)
    theirs = pl.ds(pl.multiple_of((1 - c) * half, half), half)

    loads = [
        pltpu.make_async_copy(inv_diag.at[0], inv, load_sem.at[0]),
        pltpu.make_async_copy(sources, rows, load_sem.at[1]),
        pltpu.make_async_copy(coupling.at[0, 0], blocks.at[0], load_sem.at[2]),
        pltpu.make_async_copy(coupling.at[0, 1], blocks.at[1], load_sem.at[3]),
        pltpu.make_async_copy(forward, waves.at[c], load_sem.at[4]),
    ]
    for i in (0, 1, 3, 2, 4):
        loads[i].start()

    barrier = pltpu.get_barrier_semaphore()
    for step in range(1, n):
        pl.semaphore_signal(barrier, inc=1, device_id=(lax.rem(k + step, n), g), device_id_type=MESH)
    for step in range(1, groups):
        for other in (k, peer):
            pl.semaphore_signal(barrier, inc=1, device_id=(other, lax.rem(g + step, groups)), device_id_type=MESH)

    def remote(src, dst, send, recv, chain_to, src_to):
        return pltpu.make_async_remote_copy(
            src_ref=src, dst_ref=dst, send_sem=send, recv_sem=recv,
            device_id=(chain_to, src_to), device_id_type=MESH,
        )

    def pair(i, ref):
        return remote(ref, ref, pair_send.at[i], pair_recv.at[i], peer, g)

    give_base = pair(0, base.at[c, theirs])
    take_base = pair(0, base.at[1 - c, mine])
    give_mat = [pair(1, mats.at[c, 0]), pair(2, mats.at[c, 1])]
    take_mat = [pair(1, mats.at[1 - c, 0]), pair(2, mats.at[1 - c, 1])]
    give_waves = pair(3, waves.at[c, theirs])
    take_waves = pair(3, waves.at[1 - c, mine])
    give_top = pair(4, solved.at[1])
    give_back = remote(solved.at[1 - c, mine], solved.at[1 - c, mine], back_send, back_recv, peer, g)
    take_back = remote(solved.at[c, theirs], solved.at[c, theirs], back_send, back_recv, peer, g)

    def down(panel):
        return remote(solved.at[panel, mine], above.at[panel], down_send.at[panel], down_recv.at[panel],
                      lax.max(k - 2, 0), g)

    def down_top(panel, core):
        part = pl.ds(core * half, half)
        return remote(solved.at[panel, part], above.at[panel], down_send.at[core], down_recv.at[panel],
                      lax.max(first - 2 + core, 0), g)

    def product(which):
        return (matmul(blocks[which], inv[...]) * -pattern[0, which].astype(F32)).astype(BF16)

    def overlap(panel, part):
        field = waves[panel, part].astype(F32) * solved[panel, part].astype(F32)
        return jnp.sum(field, axis=0, keepdims=True)

    loads[0].wait()
    loads[1].wait()
    base[c] = matmul(rows[...], inv[...])
    pl.semaphore_wait(barrier, n - 1 + 2 * (groups - 1))

    @pl.when(top & (c == 1))
    def _():
        solved[1] = base[1].astype(BF16)
        give_top.start()
        if n > 2:
            for core in range(2):
                down_top(1, core).start()
        loads[2].wait()
        loads[3].wait()
        loads[4].wait()
        mine_part[1] = overlap(1, slice(None))
        mine_part[0] = jnp.zeros_like(mine_part[0])

    @pl.when(top & (c == 0))
    def _():
        loads[2].wait()
        mats[0, 0] = product(0)
        give_top.wait_recv()
        solved[0] = (base[0] + matmul(solved[1], mats[0, 0])).astype(BF16)
        if n > 2:
            for core in range(2):
                down_top(0, core).start()
        loads[3].wait()
        loads[4].wait()
        mine_part[0] = overlap(0, slice(None))
        mine_part[1] = jnp.zeros_like(mine_part[1])

    @pl.when(jnp.logical_not(top))
    def _():
        give_base.start()
        loads[3].wait()
        mats[c, 1] = product(1)
        give_mat[1].start()
        loads[2].wait()
        mats[c, 0] = product(0)
        give_mat[0].start()
        loads[4].wait()
        give_waves.start()

        take_base.wait_recv()
        take_mat[1].wait_recv()
        take_mat[0].wait_recv()
        down(1).wait_recv()
        high = base[1, mine] + matmul(above[1], mats[1, 1])
        down(0).wait_recv()
        high = (high + matmul(above[0], mats[1, 0])).astype(BF16)
        solved[1, mine] = high

        @pl.when(jnp.logical_not(bottom))
        def _():
            down(1).start()

        low = base[0, mine] + matmul(above[0], mats[0, 1])
        solved[0, mine] = (low + matmul(high, mats[0, 0])).astype(BF16)

        @pl.when(jnp.logical_not(bottom))
        def _():
            down(0).start()

        take_waves.wait_recv()
        mine_part[1] = overlap(1, mine)
        mine_part[0] = overlap(0, mine)

    slot = 2 * g + c

    def part_to(step, flip):
        to = lax.rem(c + flip, 2)
        return remote(mine_part.at[to], parts.at[slot], part_send.at[2 * step + flip],
                      part_recv.at[slot], first + to, lax.rem(g + step, groups))

    def part_from(step, flip):
        owner = 2 * lax.rem(g + groups - step, groups) + lax.rem(c + flip, 2)
        return remote(mine_part.at[0], parts.at[owner], part_send.at[2 * step + flip],
                      part_recv.at[owner], peer, g)

    partners = [(step, flip) for step in range(groups) for flip in range(2) if step + flip > 0]
    for step, flip in reversed(partners):
        part_to(step, flip).start()
    parts[slot] = mine_part[c]

    @pl.when(jnp.logical_not(top))
    def _():
        give_back.start()
        take_back.wait_recv()

    store = pltpu.make_async_copy(solved.at[c], adjoint, store_sem)
    store.start()

    for step, flip in partners:
        part_from(step, flip).wait_recv()
    grad = parts[0]
    for i in range(1, 2 * groups):
        grad = grad + parts[i]
    squares[k] = jnp.broadcast_to(jnp.sum(grad * grad, axis=1, keepdims=True), (1, 128))

    def square_copy(step, owner):
        return remote(squares.at[owner], squares.at[owner], sq_send.at[step], sq_recv.at[owner],
                      lax.rem(k + step, n), g)

    for step in range(1, n):
        square_copy(step, k).start()
    for step in range(1, n):
        square_copy(step, lax.rem(k + n - step, n)).wait_recv()
    total = squares[0]
    for panel in range(1, n):
        total = total + squares[panel]
    count = float(n * grad.shape[1])
    scale = jnp.sqrt(total / count + 1e-06)
    direction[...] = grad / jnp.broadcast_to(scale[:, :1], grad.shape)

    for step, flip in partners:
        part_to(step, flip).wait_send()
    for step in range(1, n):
        square_copy(step, k).wait_send()

    @pl.when(top & (c == 1))
    def _():
        give_top.wait_send()

    if n > 2:
        @pl.when(top)
        def _():
            for core in range(2):
                down_top(c, core).wait_send()

    @pl.when(jnp.logical_not(top))
    def _():
        give_base.wait_send()
        give_mat[0].wait_send()
        give_mat[1].wait_send()
        give_waves.wait_send()
        give_back.wait_send()

        @pl.when(jnp.logical_not(bottom))
        def _():
            down(0).wait_send()
            down(1).wait_send()

    store.wait()


def solution(mesh):
    n = mesh.shape["chain"]
    groups = mesh.shape["src"]

    def per_device(sources, forward, inv_diag, coupling, pattern):
        count, width = sources.shape
        anywhere = pl.BlockSpec(memory_space=pl.ANY)
        adjoint, direction = pl.pallas_call(
            functools.partial(kernel, n, groups),
            out_shape=(
                jax.ShapeDtypeStruct((count, width), BF16),
                jax.ShapeDtypeStruct((1, width), F32),
            ),
            in_specs=[pl.BlockSpec(memory_space=pltpu.SMEM)] + [anywhere] * 4,
            out_specs=(anywhere, pl.BlockSpec(memory_space=pltpu.VMEM)),
            scratch_shapes=[
                pltpu.VMEM((count, width), BF16),
                pltpu.VMEM((2, count, width), BF16),
                pltpu.VMEM((width, width), BF16),
                pltpu.VMEM((2, width, width), BF16),
                pltpu.VMEM((2, count, width), F32),
                pltpu.VMEM((2, 2, width, width), BF16),
                pltpu.VMEM((2, count // 2, width), BF16),
                pltpu.VMEM((2, count, width), BF16),
                pltpu.VMEM((2, 1, width), F32),
                pltpu.VMEM((2 * groups, 1, width), F32),
                pltpu.VMEM((n, 1, 128), F32),
                pltpu.SemaphoreType.DMA((5,)),
                pltpu.SemaphoreType.DMA,
                pltpu.SemaphoreType.DMA((5,)),
                pltpu.SemaphoreType.DMA((5,)),
                pltpu.SemaphoreType.DMA((2,)),
                pltpu.SemaphoreType.DMA((2,)),
                pltpu.SemaphoreType.DMA,
                pltpu.SemaphoreType.DMA,
                pltpu.SemaphoreType.DMA((2 * groups,)),
                pltpu.SemaphoreType.DMA((2 * groups,)),
                pltpu.SemaphoreType.DMA((n,)),
                pltpu.SemaphoreType.DMA((n,)),
            ],
            compiler_params=pltpu.CompilerParams(
                collective_id=0, has_side_effects=True, vmem_limit_bytes=60 * 1024 * 1024
            ),
            cost_estimate=pl.CostEstimate(
                flops=2 * width * width * (2 * width + 3 * count),
                bytes_accessed=6 * width * width + 6 * count * width,
                transcendentals=0,
            ),
        )(pattern, sources, forward, inv_diag, coupling)
        return adjoint, direction.reshape(width)

    return jax.shard_map(
        per_device,
        mesh=mesh,
        in_specs=(
            P("src", "chain"),
            P("src", "chain"),
            P("chain", None, None),
            P("chain", None, None, None),
            P("chain", None),
        ),
        out_specs=(P("src", "chain"), P("chain")),
        check_vma=False,
    )
```

time: 28.2 us -> 25.9 us (0.918)
  Pallas kernels: 25.3 us -> 23 us
    pallas_call x1, Pallas kernels: 25.3 us -> 23 us  [per_device(): pl.pallas_call(functools.partial(kernel, n, groups), out_shape=(jax.Shape...]
where the time goes in v2:
time: 25.9 us; the launch traced here: 25.7 us
  Pallas kernels  23 us (89%)
  local copies, waits for them, and re-layouts  2.06 us (8%)
  between operations  0.65 us (3%)
    pallas_call x1, Pallas kernels, per_device(): pl.pallas_call(functools.partial(kernel, n, groups), out_shape=(jax.Shape...  23 us
    unnamed x4, local copies, waits for them, and re-layouts  2.06 us

profile of v2, /device:TPU:0, one launch (start us, length us, event | category | flops | bytes accessed | tf_op | source)
XLA Modules:
  0.0 25.7 jit_solution(16492320870634412595)
XLA Ops:
  0.6 23.0 %shard_map.68 = (bf16[64,512]{1,0:T(8,128)(2,1)}, f32[1,512]{1,0:T(1,128)}) custom-call(s32[1,2]{1,0:T(1,128)} %pattern.1, bf16[64,512]{1,0:T(8,128)(2,1)} %sources.1, bf16[64,512]{1,0:T(8,128)(2,1)} %forward.1, bf16[1,512,512]{2,1,0:T(8,128)(2,1)} %inv_diag.1, bf16[1,2,512,512]{3,2,1,0:T(8,128)(2,1)} %coupling.1), custom_call_target="tpu_custom_call" | custom-call | flops 637534208 | bytes 1769472 | tf_op jit(solution)/shard_map/pallas_call | solution.py:239
  23.6 0.0 copy-start
  23.7 1.5 %copy.9 = bf16[64,512]{1,0:T(8,128)(2,1)} copy(bf16[64,512]{1,0:T(8,128)(2,1)} %get-tuple-element.8) | data formatting | bytes 131072
  25.1 0.0 copy-done
  25.1 0.6 %copy.10 = f32[512]{0:T(512)} copy(f32[512]{0:T(512)S(1)} %bitcast.1) | data formatting | bytes 4096
Async XLA Ops:
  23.6 1.5 %copy-start = (f32[1,512]{1,0:T(1,128)S(1)}, f32[1,512]{1,0:T(1,128)}, u32[]{:S(2)}) copy-start(f32[1,512]{1,0:T(1,128)} %get-tuple-element.5) | copy-start | bytes 6148

commit v3 on v2

--- a/solution.py
+++ b/solution.py
@@ -18,7 +18,7 @@
 
 def kernel(n, groups, pattern, sources, forward, inv_diag, coupling, adjoint, direction,
            rows, waves, inv, blocks, base, mats, above, solved, mine_part, parts, squares,
-           load_sem, store_sem, pair_send, pair_recv, down_send, down_recv, back_send, back_recv,
+           load_sem, pair_send, pair_recv, down_send, down_recv, back_send, back_recv,
            part_send, part_recv, sq_send, sq_recv):
     k = lax.axis_index("chain")
     g = lax.axis_index("src")
@@ -173,8 +173,7 @@
         give_back.start()
         take_back.wait_recv()
 
-    store = pltpu.make_async_copy(solved.at[c], adjoint, store_sem)
-    store.start()
+    adjoint[...] = solved[c]
 
     for step, flip in partners:
         part_from(step, flip).wait_recv()
@@ -226,8 +225,6 @@
             down(0).wait_send()
             down(1).wait_send()
 
-    store.wait()
-
 
 def solution(mesh):
     n = mesh.shape["chain"]
@@ -239,11 +236,11 @@
         adjoint, direction = pl.pallas_call(
             functools.partial(kernel, n, groups),
             out_shape=(
-                jax.ShapeDtypeStruct((count, width), BF16),
-                jax.ShapeDtypeStruct((1, width), F32),
+                pltpu.VMEM((count, width), BF16),
+                pltpu.VMEM((1, width), F32),
             ),
             in_specs=[pl.BlockSpec(memory_space=pltpu.SMEM)] + [anywhere] * 4,
-            out_specs=(anywhere, pl.BlockSpec(memory_space=pltpu.VMEM)),
+            out_specs=(pl.BlockSpec(memory_space=pltpu.VMEM),) * 2,
             scratch_shapes=[
                 pltpu.VMEM((count, width), BF16),
                 pltpu.VMEM((2, count, width), BF16),
@@ -257,7 +254,6 @@
                 pltpu.VMEM((2 * groups, 1, width), F32),
                 pltpu.VMEM((n, 1, 128), F32),
                 pltpu.SemaphoreType.DMA((5,)),
-                pltpu.SemaphoreType.DMA,
                 pltpu.SemaphoreType.DMA((5,)),
                 pltpu.SemaphoreType.DMA((5,)),
                 pltpu.SemaphoreType.DMA((2,)),

time: 25.9 us -> 24.4 us (0.942)
  local copies, waits for them, and re-layouts: 2.06 us -> 1.21 us
  Pallas kernels: 23 us -> 22.4 us
    unnamed x4 -> x2, local copies, waits for them, and re-layouts: 2.06 us -> 1.21 us
    pallas_call x1, Pallas kernels: 23 us -> 22.4 us  [per_device(): pl.pallas_call(functools.partial(kernel, n, groups), out_shape=(pltpu.VME...]
where the time goes in v3:
time: 24.4 us; the launch traced here: 24.3 us
  Pallas kernels  22.4 us (92%)
  local copies, waits for them, and re-layouts  1.21 us (5%)
  between operations  0.64 us (3%)
    pallas_call x1, Pallas kernels, per_device(): pl.pallas_call(functools.partial(kernel, n, groups), out_shape=(pltpu.VME...  22.4 us
    unnamed x2, local copies, waits for them, and re-layouts  1.21 us

profile of v3, /device:TPU:0, one launch (start us, length us, event | category | flops | bytes accessed | tf_op | source)
XLA Modules:
  0.0 24.3 jit_solution(17881306411624483730)
XLA Ops:
  0.6 22.4 %shard_map.68 = (bf16[64,512]{1,0:T(8,128)(2,1)S(1)}, f32[1,512]{1,0:T(1,128)S(1)}) custom-call(s32[1,2]{1,0:T(1,128)} %pattern.1, bf16[64,512]{1,0:T(8,128)(2,1)} %sources.1, bf16[64,512]{1,0:T(8,128)(2,1)} %forward.1, bf16[1,512,512]{2,1,0:T(8,128)(2,1)} %inv_diag.1, bf16[1,2,512,512]{3,2,1,0:T(8,128)(2,1)} %coupling.1), custom_call_target="tpu_custom_call" | custom-call | flops 637534208 | bytes 1769472 | tf_op jit(solution)/shard_map/pallas_call | solution.py:236
  23.0 0.6 %copy.9 = bf16[64,512]{1,0:T(8,128)(2,1)} copy(bf16[64,512]{1,0:T(8,128)(2,1)S(1)} %get-tuple-element.6) | data formatting | bytes 131072
  23.7 0.6 %copy.10 = f32[512]{0:T(512)} copy(f32[512]{0:T(512)S(1)} %bitcast.1) | data formatting | bytes 4096

commit v4 on v3

--- a/solution.py
+++ b/solution.py
@@ -67,14 +67,24 @@
     give_back = remote(solved.at[1 - c, mine], solved.at[1 - c, mine], back_send, back_recv, peer, g)
     take_back = remote(solved.at[c, theirs], solved.at[c, theirs], back_send, back_recv, peer, g)
 
-    def down(panel):
-        return remote(solved.at[panel, mine], above.at[panel], down_send.at[panel], down_recv.at[panel],
-                      lax.max(k - 2, 0), g)
-
-    def down_top(panel, core):
+    wide = rows.shape[1] // 2
+    halves = (pl.ds(0, wide), pl.ds(wide, wide))
+
+    def down(i):
+        if i == 0:
+            src, dst = solved.at[1, mine], above.at[1]
+        else:
+            src, dst = solved.at[0, mine, halves[i - 1]], above.at[0, :, halves[i - 1]]
+        return remote(src, dst, down_send.at[i], down_recv.at[i], lax.max(k - 2, 0), g)
+
+    def down_top(i, core):
         part = pl.ds(core * half, half)
-        return remote(solved.at[panel, part], above.at[panel], down_send.at[core], down_recv.at[panel],
-                      lax.max(first - 2 + core, 0), g)
+        if i == 0:
+            src, dst, sent = solved.at[1, part], above.at[1], core
+        else:
+            src, dst = solved.at[0, part, halves[i - 1]], above.at[0, :, halves[i - 1]]
+            sent = 2 * (i - 1) + core
+        return remote(src, dst, down_send.at[sent], down_recv.at[i], lax.max(first - 2 + core, 0), g)
 
     def product(which):
         return (matmul(blocks[which], inv[...]) * -pattern[0, which].astype(F32)).astype(BF16)
@@ -94,7 +104,7 @@
         give_top.start()
         if n > 2:
             for core in range(2):
-                down_top(1, core).start()
+                down_top(0, core).start()
         loads[2].wait()
         loads[3].wait()
         loads[4].wait()
@@ -106,10 +116,11 @@
         loads[2].wait()
         mats[0, 0] = product(0)
         give_top.wait_recv()
-        solved[0] = (base[0] + matmul(solved[1], mats[0, 0])).astype(BF16)
-        if n > 2:
-            for core in range(2):
-                down_top(0, core).start()
+        for i, cols in enumerate(halves):
+            solved[0, :, cols] = (base[0, :, cols] + matmul(solved[1], mats[0, 0, :, cols])).astype(BF16)
+            if n > 2:
+                for core in range(2):
+                    down_top(1 + i, core).start()
         loads[3].wait()
         loads[4].wait()
         mine_part[0] = overlap(0, slice(None))
@@ -130,26 +141,37 @@
         take_base.wait_recv()
         take_mat[1].wait_recv()
         take_mat[0].wait_recv()
+        take_waves.wait_recv()
+
+    def solve(last):
+        down(0).wait_recv()
+        high = base[1, mine] + matmul(above[1], mats[1, 1])
         down(1).wait_recv()
-        high = base[1, mine] + matmul(above[1], mats[1, 1])
-        down(0).wait_recv()
-        high = (high + matmul(above[0], mats[1, 0])).astype(BF16)
+        left = above[0, :, halves[0]]
+        high = high + matmul(left, mats[1, 0, halves[0]])
+        low = base[0, mine] + matmul(left, mats[0, 1, halves[0]])
+        down(2).wait_recv()
+        right = above[0, :, halves[1]]
+        high = (high + matmul(right, mats[1, 0, halves[1]])).astype(BF16)
         solved[1, mine] = high
-
-        @pl.when(jnp.logical_not(bottom))
-        def _():
-            down(1).start()
-
-        low = base[0, mine] + matmul(above[0], mats[0, 1])
-        solved[0, mine] = (low + matmul(high, mats[0, 0])).astype(BF16)
-
-        @pl.when(jnp.logical_not(bottom))
-        def _():
+        if not last:
             down(0).start()
-
-        take_waves.wait_recv()
+        low = low + matmul(right, mats[0, 1, halves[1]])
+        for i, cols in enumerate(halves):
+            piece = low[:, i * wide:(i + 1) * wide] + matmul(high, mats[0, 0, :, cols])
+            solved[0, mine, cols] = piece.astype(BF16)
+            if not last:
+                down(1 + i).start()
         mine_part[1] = overlap(1, mine)
         mine_part[0] = overlap(0, mine)
+
+    @pl.when(bottom & jnp.logical_not(top))
+    def _():
+        solve(True)
+
+    @pl.when(jnp.logical_not(bottom | top))
+    def _():
+        solve(False)
 
     slot = 2 * g + c
 
@@ -186,7 +208,7 @@
         return remote(squares.at[owner], squares.at[owner], sq_send.at[step], sq_recv.at[owner],
                       lax.rem(k + step, n), g)
 
-    for step in range(1, n):
+    for step in reversed(range(1, n)):
         square_copy(step, k).start()
     for step in range(1, n):
         square_copy(step, lax.rem(k + n - step, n)).wait_recv()
@@ -207,10 +229,16 @@
         give_top.wait_send()
 
     if n > 2:
-        @pl.when(top)
+        @pl.when(top & (c == 1))
         def _():
             for core in range(2):
-                down_top(c, core).wait_send()
+                down_top(0, core).wait_send()
+
+        @pl.when(top & (c == 0))
+        def _():
+            for core in range(2):
+                down_top(1, core).wait_send()
+                down_top(2, core).wait_send()
 
     @pl.when(jnp.logical_not(top))
     def _():
@@ -222,8 +250,8 @@
 
         @pl.when(jnp.logical_not(bottom))
         def _():
-            down(0).wait_send()
-            down(1).wait_send()
+            for i in range(3):
+                down(i).wait_send()
 
 
 def solution(mesh):
@@ -256,8 +284,8 @@
                 pltpu.SemaphoreType.DMA((5,)),
                 pltpu.SemaphoreType.DMA((5,)),
                 pltpu.SemaphoreType.DMA((5,)),
-                pltpu.SemaphoreType.DMA((2,)),
-                pltpu.SemaphoreType.DMA((2,)),
+                pltpu.SemaphoreType.DMA((4,)),
+                pltpu.SemaphoreType.DMA((3,)),
                 pltpu.SemaphoreType.DMA,
                 pltpu.SemaphoreType.DMA,
                 pltpu.SemaphoreType.DMA((2 * groups,)),

time: 24.4 us -> 24.3 us (level)
  no operation moved by 1% of the time
where the time goes in v4:
time: 24.3 us; the launch traced here: 24.1 us
  Pallas kernels  22.3 us (92%)
  local copies, waits for them, and re-layouts  1.21 us (5%)
  between operations  0.64 us (3%)
    pallas_call x1, Pallas kernels, per_device(): pl.pallas_call(functools.partial(kernel, n, groups), out_shape=(pltpu.VME...  22.3 us
    unnamed x2, local copies, waits for them, and re-layouts  1.21 us

profile of v4, /device:TPU:0, one launch (start us, length us, event | category | flops | bytes accessed | tf_op | source)
XLA Modules:
  0.0 24.1 jit_solution(489029687592696282)
XLA Ops:
  0.6 22.3 %shard_map.68 = (bf16[64,512]{1,0:T(8,128)(2,1)S(1)}, f32[1,512]{1,0:T(1,128)S(1)}) custom-call(s32[1,2]{1,0:T(1,128)} %pattern.1, bf16[64,512]{1,0:T(8,128)(2,1)} %sources.1, bf16[64,512]{1,0:T(8,128)(2,1)} %forward.1, bf16[1,512,512]{2,1,0:T(8,128)(2,1)} %inv_diag.1, bf16[1,2,512,512]{3,2,1,0:T(8,128)(2,1)} %coupling.1), custom_call_target="tpu_custom_call" | custom-call | flops 637534208 | bytes 1769472 | tf_op jit(solution)/shard_map/pallas_call | solution.py:264
  22.9 0.6 %copy.9 = bf16[64,512]{1,0:T(8,128)(2,1)} copy(bf16[64,512]{1,0:T(8,128)(2,1)S(1)} %get-tuple-element.6) | data formatting | bytes 131072
  23.6 0.6 %copy.10 = f32[512]{0:T(512)} copy(f32[512]{0:T(512)S(1)} %bitcast.1) | data formatting | bytes 4096

commit v5 on v4

--- a/solution.py
+++ b/solution.py
@@ -17,15 +17,17 @@
 
 
 def kernel(n, groups, pattern, sources, forward, inv_diag, coupling, adjoint, direction,
-           rows, waves, inv, blocks, base, mats, above, solved, mine_part, parts, squares,
-           load_sem, pair_send, pair_recv, down_send, down_recv, back_send, back_recv,
+           rows, waves, inv, blocks, base, mats, above, whole, solved, mine_part, parts, squares,
+           load_sem, pair_send, pair_recv, down_send, down_recv, whole_recv, back_send, back_recv,
            part_send, part_recv, sq_send, sq_recv):
     k = lax.axis_index("chain")
     g = lax.axis_index("src")
     c = lax.rem(k, 2)
     first = k - c
     peer = first + 1 - c
+    relay = n >= 6
     top = k >= n - 2
+    owner = k >= (n - 4 if relay else n - 2)
     bottom = k < 2
     half = rows.shape[0] // 2
     mine = pl.ds(pl.multiple_of(c * half, half), half)
@@ -86,6 +88,31 @@
             sent = 2 * (i - 1) + core
         return remote(src, dst, down_send.at[sent], down_recv.at[i], lax.max(first - 2 + core, 0), g)
 
+    def down_whole(i):
+        if i == 0:
+            src, dst = solved.at[1], whole.at[1]
+        else:
+            src, dst = solved.at[0, :, halves[i - 1]], whole.at[0, :, halves[i - 1]]
+        return remote(src, dst, down_send.at[i], whole_recv.at[i], lax.max(first - 1, 0), g)
+
+    onward = pair(0, whole.at[0])
+
+    def send_down(i):
+        if n <= 2:
+            return
+        if relay:
+            @pl.when(top)
+            def _():
+                down_whole(i).start()
+
+            @pl.when(jnp.logical_not(top))
+            def _():
+                for core in range(2):
+                    down_top(i, core).start()
+        else:
+            for core in range(2):
+                down_top(i, core).start()
+
     def product(which):
         return (matmul(blocks[which], inv[...]) * -pattern[0, which].astype(F32)).astype(BF16)
 
@@ -101,32 +128,58 @@
     @pl.when(top & (c == 1))
     def _():
         solved[1] = base[1].astype(BF16)
+
+    if relay:
+        @pl.when(owner & jnp.logical_not(top) & (c == 1))
+        def _():
+            loads[3].wait()
+            mats[1, 1] = product(1)
+            loads[2].wait()
+            mats[1, 0] = product(0)
+            down_whole(0).wait_recv()
+            high = base[1] + matmul(whole[1], mats[1, 1])
+            down_whole(1).wait_recv()
+            high = high + matmul(whole[0, :, halves[0]], mats[1, 0, halves[0]])
+            down_whole(2).wait_recv()
+            onward.start()
+            solved[1] = (high + matmul(whole[0, :, halves[1]], mats[1, 0, halves[1]])).astype(BF16)
+
+    @pl.when(owner & (c == 1))
+    def _():
         give_top.start()
-        if n > 2:
-            for core in range(2):
-                down_top(0, core).start()
-        loads[2].wait()
-        loads[3].wait()
+        send_down(0)
+
+        @pl.when(top)
+        def _():
+            loads[2].wait()
+            loads[3].wait()
+
         loads[4].wait()
         mine_part[1] = overlap(1, slice(None))
         mine_part[0] = jnp.zeros_like(mine_part[0])
 
-    @pl.when(top & (c == 0))
+    @pl.when(owner & (c == 0))
     def _():
         loads[2].wait()
         mats[0, 0] = product(0)
+        loads[3].wait()
+
+        if relay:
+            @pl.when(jnp.logical_not(top))
+            def _():
+                mats[0, 1] = product(1)
+                onward.wait_recv()
+                base[0] += matmul(whole[0], mats[0, 1])
+
         give_top.wait_recv()
         for i, cols in enumerate(halves):
             solved[0, :, cols] = (base[0, :, cols] + matmul(solved[1], mats[0, 0, :, cols])).astype(BF16)
-            if n > 2:
-                for core in range(2):
-                    down_top(1 + i, core).start()
-        loads[3].wait()
+            send_down(1 + i)
         loads[4].wait()
         mine_part[0] = overlap(0, slice(None))
         mine_part[1] = jnp.zeros_like(mine_part[1])
 
-    @pl.when(jnp.logical_not(top))
+    @pl.when(jnp.logical_not(owner))
     def _():
         give_base.start()
         loads[3].wait()
@@ -165,11 +218,11 @@
         mine_part[1] = overlap(1, mine)
         mine_part[0] = overlap(0, mine)
 
-    @pl.when(bottom & jnp.logical_not(top))
+    @pl.when(bottom & jnp.logical_not(owner))
     def _():
         solve(True)
 
-    @pl.when(jnp.logical_not(bottom | top))
+    @pl.when(jnp.logical_not(bottom | owner))
     def _():
         solve(False)
 
@@ -190,7 +243,7 @@
         part_to(step, flip).start()
     parts[slot] = mine_part[c]
 
-    @pl.when(jnp.logical_not(top))
+    @pl.when(jnp.logical_not(owner))
     def _():
         give_back.start()
         take_back.wait_recv()
@@ -224,23 +277,38 @@
     for step in range(1, n):
         square_copy(step, k).wait_send()
 
-    @pl.when(top & (c == 1))
+    @pl.when(owner & (c == 1))
     def _():
         give_top.wait_send()
 
-    if n > 2:
-        @pl.when(top & (c == 1))
-        def _():
-            for core in range(2):
-                down_top(0, core).wait_send()
-
-        @pl.when(top & (c == 0))
-        def _():
-            for core in range(2):
-                down_top(1, core).wait_send()
-                down_top(2, core).wait_send()
-
-    @pl.when(jnp.logical_not(top))
+    def sent_down(items):
+        if relay:
+            @pl.when(top)
+            def _():
+                for i in items:
+                    down_whole(i).wait_send()
+
+        if n > 2:
+            @pl.when(jnp.logical_not(top) if relay else top)
+            def _():
+                for i in items:
+                    for core in range(2):
+                        down_top(i, core).wait_send()
+
+    @pl.when(owner & (c == 1))
+    def _():
+        sent_down((0,))
+
+        if relay:
+            @pl.when(jnp.logical_not(top))
+            def _():
+                onward.wait_send()
+
+    @pl.when(owner & (c == 0))
+    def _():
+        sent_down((1, 2))
+
+    @pl.when(jnp.logical_not(owner))
     def _():
         give_base.wait_send()
         give_mat[0].wait_send()
@@ -278,6 +346,7 @@
                 pltpu.VMEM((2, 2, width, width), BF16),
                 pltpu.VMEM((2, count // 2, width), BF16),
                 pltpu.VMEM((2, count, width), BF16),
+                pltpu.VMEM((2, count, width), BF16),
                 pltpu.VMEM((2, 1, width), F32),
                 pltpu.VMEM((2 * groups, 1, width), F32),
                 pltpu.VMEM((n, 1, 128), F32),
@@ -285,6 +354,7 @@
                 pltpu.SemaphoreType.DMA((5,)),
                 pltpu.SemaphoreType.DMA((5,)),
                 pltpu.SemaphoreType.DMA((4,)),
+                pltpu.SemaphoreType.DMA((3,)),
                 pltpu.SemaphoreType.DMA((3,)),
                 pltpu.SemaphoreType.DMA,
                 pltpu.SemaphoreType.DMA,

time: 24.3 us -> 25.2 us (1.037)
  Pallas kernels: 22.3 us -> 23.2 us
    pallas_call x1, Pallas kernels: 22.3 us -> 23.2 us  [per_device(): pl.pallas_call(functools.partial(kernel, n, groups), out_shape=(pltpu.VME...]
where the time goes in v5:
time: 25.2 us; the launch traced here: 25 us
  Pallas kernels  23.2 us (92%)
  local copies, waits for them, and re-layouts  1.21 us (5%)
  between operations  0.64 us (3%)
    pallas_call x1, Pallas kernels, per_device(): pl.pallas_call(functools.partial(kernel, n, groups), out_shape=(pltpu.VME...  23.2 us
    unnamed x2, local copies, waits for them, and re-layouts  1.21 us

profile of v5, /device:TPU:0, one launch (start us, length us, event | category | flops | bytes accessed | tf_op | source)
XLA Modules:
  0.0 25.0 jit_solution(10130239813621711436)
XLA Ops:
  0.6 23.2 %shard_map.68 = (bf16[64,512]{1,0:T(8,128)(2,1)S(1)}, f32[1,512]{1,0:T(1,128)S(1)}) custom-call(s32[1,2]{1,0:T(1,128)} %pattern.1, bf16[64,512]{1,0:T(8,128)(2,1)} %sources.1, bf16[64,512]{1,0:T(8,128)(2,1)} %forward.1, bf16[1,512,512]{2,1,0:T(8,128)(2,1)} %inv_diag.1, bf16[1,2,512,512]{3,2,1,0:T(8,128)(2,1)} %coupling.1), custom_call_target="tpu_custom_call" | custom-call | flops 637534208 | bytes 1769472 | tf_op jit(solution)/shard_map/pallas_call | solution.py:332
  23.8 0.6 %copy.9 = bf16[64,512]{1,0:T(8,128)(2,1)} copy(bf16[64,512]{1,0:T(8,128)(2,1)S(1)} %get-tuple-element.6) | data formatting | bytes 131072
  24.4 0.6 %copy.10 = f32[512]{0:T(512)} copy(f32[512]{0:T(512)S(1)} %bitcast.1) | data formatting | bytes 4096

commit v6 on v4

--- a/solution.py
+++ b/solution.py
@@ -38,15 +38,15 @@
         pltpu.make_async_copy(coupling.at[0, 1], blocks.at[1], load_sem.at[3]),
         pltpu.make_async_copy(forward, waves.at[c], load_sem.at[4]),
     ]
-    for i in (0, 1, 3, 2, 4):
-        loads[i].start()
-
     barrier = pltpu.get_barrier_semaphore()
     for step in range(1, n):
         pl.semaphore_signal(barrier, inc=1, device_id=(lax.rem(k + step, n), g), device_id_type=MESH)
     for step in range(1, groups):
         for other in (k, peer):
             pl.semaphore_signal(barrier, inc=1, device_id=(other, lax.rem(g + step, groups)), device_id_type=MESH)
+
+    for i in (0, 1, 3, 2, 4):
+        loads[i].start()
 
     def remote(src, dst, send, recv, chain_to, src_to):
         return pltpu.make_async_remote_copy(
@@ -193,9 +193,6 @@
     @pl.when(jnp.logical_not(top))
     def _():
         give_back.start()
-        take_back.wait_recv()
-
-    adjoint[...] = solved[c]
 
     for step, flip in partners:
         part_from(step, flip).wait_recv()
@@ -210,6 +207,12 @@
 
     for step in reversed(range(1, n)):
         square_copy(step, k).start()
+
+    @pl.when(jnp.logical_not(top))
+    def _():
+        take_back.wait_recv()
+
+    adjoint[...] = solved[c]
     for step in range(1, n):
         square_copy(step, lax.rem(k + n - step, n)).wait_recv()
     total = squares[0]

time: 24.3 us -> 24.4 us (level)
  no operation moved by 1% of the time
where the time goes in v6:
time: 24.4 us; the launch traced here: 24.3 us
  Pallas kernels  22.4 us (92%)
  local copies, waits for them, and re-layouts  1.21 us (5%)
  between operations  0.64 us (3%)
    pallas_call x1, Pallas kernels, per_device(): pl.pallas_call(functools.partial(kernel, n, groups), out_shape=(pltpu.VME...  22.4 us
    unnamed x2, local copies, waits for them, and re-layouts  1.21 us

profile of v6, /device:TPU:0, one launch (start us, length us, event | category | flops | bytes accessed | tf_op | source)
XLA Modules:
  0.0 24.3 jit_solution(7412290918076263848)
XLA Ops:
  0.6 22.4 %shard_map.68 = (bf16[64,512]{1,0:T(8,128)(2,1)S(1)}, f32[1,512]{1,0:T(1,128)S(1)}) custom-call(s32[1,2]{1,0:T(1,128)} %pattern.1, bf16[64,512]{1,0:T(8,128)(2,1)} %sources.1, bf16[64,512]{1,0:T(8,128)(2,1)} %forward.1, bf16[1,512,512]{2,1,0:T(8,128)(2,1)} %inv_diag.1, bf16[1,2,512,512]{3,2,1,0:T(8,128)(2,1)} %coupling.1), custom_call_target="tpu_custom_call" | custom-call | flops 637534208 | bytes 1769472 | tf_op jit(solution)/shard_map/pallas_call | solution.py:267
  23.1 0.6 %copy.9 = bf16[64,512]{1,0:T(8,128)(2,1)} copy(bf16[64,512]{1,0:T(8,128)(2,1)S(1)} %get-tuple-element.6) | data formatting | bytes 131072
  23.7 0.6 %copy.10 = f32[512]{0:T(512)} copy(f32[512]{0:T(512)S(1)} %bitcast.1) | data formatting | bytes 4096
